TPU v7x, 512 devices: a whole 4x4x16 slice. The times are simulated.
512 devices in a mesh: rows: 128 (over y_hi, x, z), cols: 4 (over y_lo, core).
Axes of the slice: x: 4, y: 4 (y_hi: 2, y_lo: 2; y = y_hi * 2 + y_lo), z: 16, core: 2. Of those that a mesh axis runs over, the one named last changes fastest.
Arguments:
- design_panel: float32 [128, 524288], P('cols', 'rows')
- sign_bits: int32 [524288], P('rows'), may hold values from 0 to 1
- sample_rows: int32 [512], replicated, may hold values from 0 to 524287
Outputs:
- conditioned: float32 [128, 524288], P('cols', 'rows')
All inputs are finite; a program needn't handle non-finite values.
Results may differ from a plain program's by a relative error of at most 0.00015.
Values sent between devices are 32-bit elements; how exact they have to be, the bound alone decides.
A program may use at most 64 MiB of HBM per device.

v0:
```python
import jax
import jax.numpy as jnp
from jax import lax
from jax.sharding import PartitionSpec as P

precise = lax.Precision.HIGHEST


def swapped(value, axis, distance):
    mask = 2**distance
    pairs = [(source, source ^ mask) for source in range(lax.axis_size(axis))]
    return lax.ppermute(value, axis, pairs)


def sylvester(length):
    indices = jnp.arange(length, dtype=jnp.int32)
    common_bits = indices[:, None] & indices[None, :]
    parity = jnp.zeros((length, length), jnp.int32)
    for level in range(length.bit_length() - 1):
        parity = parity ^ common_bits >> level & 1
    return (1 - 2 * parity).astype(jnp.float32)


def shards(design_panel, sign_bits, sample_rows):
    local_cols, rows_here = design_panel.shape
    devices = lax.axis_size("rows")
    blocks = rows_here // devices
    total_rows = rows_here * devices
    outer_table = sylvester(devices)
    inner_table = sylvester(blocks)
    flipped = design_panel * (2 * sign_bits - 1).astype(jnp.float32)[None, :]
    cube_view = flipped.reshape(local_cols, devices, blocks)
    inner_done = jnp.einsum("cjm,mn->ncj", cube_view, inner_table, precision=precise)
    local_mixed = jnp.einsum("ncj,jk->nck", inner_done, outer_table, precision=precise)
    current = local_mixed
    my_index = lax.axis_index("rows")
    for level in range(devices.bit_length() - 1):
        partner = swapped(current, "rows", level)
        upper_half = my_index >> level & 1 == 1
        current = jnp.where(upper_half, partner - current, current + partner)
    mixed_cube = current
    mixed_cube = mixed_cube * (1.0 / jnp.sqrt(jnp.float32(total_rows)))
    mixed_panel = mixed_cube.transpose(1, 2, 0).reshape(local_cols, rows_here)
    row_start = lax.axis_index("rows") * rows_here
    offsets = sample_rows - row_start
    owned_mask = ((offsets >= 0) & (offsets < rows_here)).astype(jnp.float32)
    picked = (
        jnp.take(mixed_panel, jnp.clip(offsets, 0, rows_here - 1), axis=1) * owned_mask[None, :]
    )
    sample_count = sample_rows.shape[0]
    full_samples = lax.all_gather(picked, "cols", axis=0, tiled=True)
    partial_gram = jnp.dot(full_samples, full_samples.T, precision=precise)
    gram_matrix = lax.psum(partial_gram, "rows") / sample_count
    lower_factor = jnp.linalg.cholesky(gram_matrix)
    identity = jnp.eye(gram_matrix.shape[0], dtype=jnp.float32)
    inverse = lax.linalg.triangular_solve(lower_factor, identity, left_side=True, lower=True)
    my_first = lax.axis_index("cols") * local_cols
    my_inverse = lax.dynamic_slice_in_dim(inverse, my_first, local_cols, 0)
    return jnp.dot(
        my_inverse, lax.all_gather(mixed_panel, "cols", axis=0, tiled=True), precision=precise
    )


def solution(mesh):
    in_specs = (P("cols", "rows"), P("rows"), P())
    out_specs = P("cols", "rows")
    return jax.shard_map(shards, mesh=mesh, in_specs=in_specs, out_specs=out_specs, check_vma=False)
```

profile of v0, /device:TPU:1, one launch (start us, length us, event | category | flops | bytes accessed | tf_op | source)
XLA Modules:
  0.0 1413.7 jit_solution(1593301636862965995)
XLA Ops:
  7.4 0.7 add_convert_fusion
  8.1 1.1 broadcast_multiply_fusion
  9.2 0.7 reshape.22
  9.9 2.2 fusion.40
  12.1 0.9 fusion
  13.0 4.4 collective-permute-start
  17.4 7.0 collective-permute-done
  24.4 0.1 add_select_fusion.5
  24.5 9.4 collective-permute-start.1
  33.9 22.6 %collective-permute-done.1 = f32[32,32,128]{2,1,0:T(8,128)S(1)} collective-permute-done((f32[32,32,128]{2,1,0:T(8,128)S(1)}, f32[32,32,128]{2,1,0:T(8,128)S(1)}, u32[]{:S(2)}, u32[]{:S(2)}) %collective-permute-start.1) | collective-permute-done | bytes 524320 | tf_op jit(solution)/shard_map/ppermute | solution.py:12
  56.5 0.1 add_select_fusion.4
  56.6 8.8 collective-permute-start.2
  65.4 45.1 %collective-permute-done.2 = f32[32,32,128]{2,1,0:T(8,128)S(1)} collective-permute-done((f32[32,32,128]{2,1,0:T(8,128)S(1)}, f32[32,32,128]{2,1,0:T(8,128)S(1)}, u32[]{:S(2)}, u32[]{:S(2)}) %collective-permute-start.2) | collective-permute-done | bytes 524320 | tf_op jit(solution)/shard_map/ppermute | solution.py:12
  110.5 0.1 add_select_fusion.3
  110.6 24.3 %collective-permute-start.3 = (f32[32,32,128]{2,1,0:T(8,128)S(1)}, f32[32,32,128]{2,1,0:T(8,128)S(1)}, u32[]{:S(2)}, u32[]{:S(2)}) collective-permute-start(f32[32,32,128]{2,1,0:T(8,128)S(1)} %add_select_fusion.3), channel_id=1, source_target_pairs={{0,32},{4,36},{8,40},{12,44},{16,48},{20,52},{24,56},{28,60},{32,0... | collective-permute-start | bytes 1572872 | tf_op jit(solution)/shard_map/ppermute | solution.py:12
  134.9 17.6 %collective-permute-done.3 = f32[32,32,128]{2,1,0:T(8,128)S(1)} collective-permute-done((f32[32,32,128]{2,1,0:T(8,128)S(1)}, f32[32,32,128]{2,1,0:T(8,128)S(1)}, u32[]{:S(2)}, u32[]{:S(2)}) %collective-permute-start.3) | collective-permute-done | bytes 524320 | tf_op jit(solution)/shard_map/ppermute | solution.py:12
  152.4 0.1 add_select_fusion.2
  152.5 3.1 collective-permute-start.4
  155.7 11.8 collective-permute-done.4
  167.4 0.1 add_select_fusion.1
  167.5 4.6 collective-permute-start.5
  172.2 10.8 collective-permute-done.5
  183.0 0.1 add_select_fusion
  183.1 4.8 collective-permute-start.6
  187.9 9.7 collective-permute-done.6
  197.6 0.1 multiply_bitcast_fusion
  197.7 0.6 copy.12
  198.3 1.0 reshape.23
  199.3 0.6 copy.13
  199.9 1.0 gather_fusion
  201.0 0.2 multiply_bitcast_fusion.1
  201.2 0.1 copy.14
  201.3 8.9 all_gather.6
  210.1 1.0 fusion.82
  211.1 0.0 all-reduce.2.cloned.1.call-update
  211.1 0.2 all-gather.2.cloned.1.call-start
  211.4 0.3 all-gather.2.cloned.1.call-update
  211.7 1165.9 %all-reduce.2.cloned.1.call-done = f32[128,128]{0,1:T(8,128)} async-done(((f32[128,128]{0,1:T(8,128)}), f32[128,128]{0,1:T(8,128)}) %all-reduce.2.cloned.1.call-update) | async-done | bytes 65552 | tf_op jit(solution)/shard_map/psum | solution.py:53
  1377.6 0.8 broadcast_multiply_fusion.1
  1378.5 0.1 copy.16
  1378.6 0.9 fusion.5
  1379.4 11.7 cholesky.17
  1391.2 0.7 compare_reduce_fusion
  1391.9 0.7 fusion.2
  1392.6 9.8 custom-call.6
  1402.4 0.2 fusion.3
  1402.6 0.0 all-gather.2.cloned.1.call-done
  1402.7 3.6 fusion.42
  (8 shorter events, 0.1 us)
Async XLA Ops:
  7.4 1370.3 %all-reduce.2.cloned.1.call-start = ((), (), s32[]{:S(2)}) async-start(), calls=%async_computation | async-start | bytes 131072 | tf_op jit(solution)/shard_map/psum | solution.py:53
  13.0 11.4 collective-permute-start
  24.5 32.0 %collective-permute-start.1 = (f32[32,32,128]{2,1,0:T(8,128)S(1)}, f32[32,32,128]{2,1,0:T(8,128)S(1)}, u32[]{:S(2)}, u32[]{:S(2)}) collective-permute-start(f32[32,32,128]{2,1,0:T(8,128)S(1)} %add_select_fusion.5), channel_id=1, source_target_pairs={{0,8},{4,12},{8,0},{12,4},{16,24},{20,28},{24,16},{28,20},{32,40},... | collective-permute-start | bytes 1572872 | tf_op jit(solution)/shard_map/ppermute | solution.py:12
  56.6 53.9 %collective-permute-start.2 = (f32[32,32,128]{2,1,0:T(8,128)S(1)}, f32[32,32,128]{2,1,0:T(8,128)S(1)}, u32[]{:S(2)}, u32[]{:S(2)}) collective-permute-start(f32[32,32,128]{2,1,0:T(8,128)S(1)} %add_select_fusion.4), channel_id=1, source_target_pairs={{0,16},{4,20},{8,24},{12,28},{16,0},{20,4},{24,8},{28,12},{32,48},... | collective-permute-start | bytes 1572872 | tf_op jit(solution)/shard_map/ppermute | solution.py:12
  110.6 41.9 %collective-permute-start.3 = (f32[32,32,128]{2,1,0:T(8,128)S(1)}, f32[32,32,128]{2,1,0:T(8,128)S(1)}, u32[]{:S(2)}, u32[]{:S(2)}) collective-permute-start(f32[32,32,128]{2,1,0:T(8,128)S(1)} %add_select_fusion.3), channel_id=1, source_target_pairs={{0,32},{4,36},{8,40},{12,44},{16,48},{20,52},{24,56},{28,60},{32,0... | collective-permute-start | bytes 1572872 | tf_op jit(solution)/shard_map/ppermute | solution.py:12
  134.9 53.0 %copy-start.1 = (s32[512]{0:T(512)S(1)}, s32[512]{0:T(512)}, u32[]{:S(2)}) copy-start(s32[512]{0:T(512)} %param.5) | copy-start | bytes 6148
  152.5 14.9 %collective-permute-start.4 = (f32[32,32,128]{2,1,0:T(8,128)S(1)}, f32[32,32,128]{2,1,0:T(8,128)S(1)}, u32[]{:S(2)}, u32[]{:S(2)}) collective-permute-start(f32[32,32,128]{2,1,0:T(8,128)S(1)} %add_select_fusion.2), channel_id=1, source_target_pairs={{0,64},{4,68},{8,72},{12,76},{16,80},{20,84},{24,88},{28,92},{32,9... | collective-permute-start | bytes 1572872 | tf_op jit(solution)/shard_map/ppermute | solution.py:12
  167.5 15.5 %collective-permute-start.5 = (f32[32,32,128]{2,1,0:T(8,128)S(1)}, f32[32,32,128]{2,1,0:T(8,128)S(1)}, u32[]{:S(2)}, u32[]{:S(2)}) collective-permute-start(f32[32,32,128]{2,1,0:T(8,128)S(1)} %add_select_fusion.1), channel_id=1, source_target_pairs={{0,128},{4,132},{8,136},{12,140},{16,144},{20,148},{24,152},{28,15... | collective-permute-start | bytes 1572872 | tf_op jit(solution)/shard_map/ppermute | solution.py:12
  183.1 14.5 %collective-permute-start.6 = (f32[32,32,128]{2,1,0:T(8,128)S(1)}, f32[32,32,128]{2,1,0:T(8,128)S(1)}, u32[]{:S(2)}, u32[]{:S(2)}) collective-permute-start(f32[32,32,128]{2,1,0:T(8,128)S(1)} %add_select_fusion), channel_id=1, source_target_pairs={{0,256},{4,260},{8,264},{12,268},{16,272},{20,276},{24,280},{28,28... | collective-permute-start | bytes 1572872 | tf_op jit(solution)/shard_map/ppermute | solution.py:12
  199.3 10.8 copy-start
  211.1 1191.5 %all-gather.2.cloned.1.call-start = ((), (), s32[]{:S(2)}) async-start(), calls=%async_computation.1 | async-start | bytes 2621440 | tf_op jit(solution)/shard_map/all_gather | solution.py:60
Sparse Core Ops, SparseCore 0:
  211.3 1166.3 all-reduce.1
Sparse Core Ops, SparseCore 1:
  213.7 48.8 all-gather.1
where the time goes:
time: 1440 us; the launch traced here: 1410 us
  waiting for transfers between devices  1290 us (90%)
  starting transfers between devices  59.6 us (4%)
  other arithmetic  27.3 us (2%)
  between operations  15.1 us (1%)
    psum x1, waiting for transfers between devices, shards(): gram_matrix = lax.psum(partial_gram, 'rows') / sample_count  1170 us
    ppermute x7, waiting for transfers between devices, swapped(): return lax.ppermute(value, axis, pairs)  124 us
    ppermute x7, starting transfers between devices, swapped(): return lax.ppermute(value, axis, pairs)  59.4 us
  transfers between devices with their start and end apart: 9, of which 8 were waited for; matrix products, arithmetic and copies ran while one was open for 2% of the time, Pallas kernels for 0%

commit v1 on v0

v1 whole, which is shorter than its diff:
```python
import functools
import math

import jax
import jax.numpy as jnp
from jax import lax
from jax.experimental import pallas as pl
from jax.experimental.pallas import tpu as pltpu
from jax.sharding import PartitionSpec as P

MESH = pl.DeviceIdType.MESH
f32, bf16, i32 = jnp.float32, jnp.bfloat16, jnp.int32
HIGH = lax.Precision.HIGHEST
N_X, N_Z = 4, 16
PLANE = 8


def parity(value, bits):
    shift = bits // 2
    while shift:
        value = value ^ (value >> shift)
        shift //= 2
    return value & 1


def sylvester(n):
    rows = lax.broadcasted_iota(i32, (n, n), 0)
    cols = lax.broadcasted_iota(i32, (n, n), 1)
    return (1 - 2 * parity(rows & cols, 8)).astype(f32).astype(bf16)


def parts(value):
    high = value.astype(bf16)
    rest = value - high.astype(f32)
    middle = rest.astype(bf16)
    low = (rest - middle.astype(f32)).astype(bf16)
    return high, middle, low


def exact_dot(value, table):
    high, middle, low = parts(value)
    dot = functools.partial(jnp.dot, preferred_element_type=f32)
    return dot(low, table) + dot(middle, table) + dot(high, table)


def butterflies(tiles):
    n = tiles.shape[0]
    half = 1
    while half < n:
        pairs = tiles.reshape(n // (2 * half), 2, half, 8, 128)
        a, b = pairs[:, 0], pairs[:, 1]
        tiles = jnp.stack([a + b, a - b], axis=1).reshape(n, 8, 128)
        half *= 2
    return tiles


def wait_bytes(ref, sem):
    pltpu.make_async_copy(ref, ref, sem).wait()


def kernel(
    x_ref, sign_ref, sample_ref, out_ref,
    local, first, mixed, second, result,
    pick, pick_in, zsum, zsum_in, zrow, zall, picked, picked_all, factor,
    send_first, recv_first, send_second, recv_second, send_out, recv_out,
    chain_send, chain_recv, local_sem,
):
    p = lax.axis_index("rows")
    a = lax.axis_index("cols")
    z = lax.rem(p, N_Z)
    x = lax.rem(lax.div(p, N_Z), N_X)
    y = lax.div(p, N_Z * N_X)
    e = y * N_X + x
    quarter = lax.rem(x, 2) * 2 + lax.div(z, 8)
    slot = lax.rem(z, 8)
    block = y * 2 + lax.div(x, 2)

    def row_at(dz, de):
        zz = lax.rem(z + dz, N_Z)
        xx = lax.rem(x + lax.rem(de, N_X), N_X)
        yy = lax.rem(y + lax.div(de, N_X), 2)
        return (yy * N_X + xx) * N_Z + zz, yy * N_X + xx, zz

    def order(k):
        half = lax.rem(k, 2)
        de = lax.rem(lax.div(k, 2), PLANE)
        dz = lax.rem(3 * lax.div(k, 16), 8) + 8 * half
        return dz, de

    scale = f32(1.0 / math.sqrt(524288.0))
    signs = (2 * sign_ref[...] - 1).astype(f32) * scale
    table = sylvester(128)
    for cb in range(4):
        flipped = x_ref[cb * 8 : cb * 8 + 8, :] * signs
        tiles = jnp.concatenate([flipped[:, j * 128 : j * 128 + 128] for j in range(32)], axis=0)
        tiles = exact_dot(tiles, table).reshape(32, 8, 128)
        local[cb * 32 : cb * 32 + 32] = butterflies(tiles)

    def send_tile(k, carry):
        dz, de = order(k)
        row, _, _ = row_at(dz, de)
        pltpu.make_async_remote_copy(
            src_ref=local.at[row], dst_ref=first.at[p], send_sem=send_first, recv_sem=recv_first,
            device_id=(row, a), device_id_type=MESH,
        ).start()
        return carry

    lax.fori_loop(1, 128, send_tile, 0)
    first[p] = local[p]

    samples = sample_ref[...]
    hot = (lax.broadcasted_iota(i32, (128, 512), 0) == lax.rem(samples, 128)).astype(f32).astype(bf16)
    want = jnp.broadcast_to(lax.rem(lax.div(samples, 128), 32), (8, 512))
    flip = (1 - 2 * parity(lax.div(samples, 4096) & p, 8)).astype(f32)
    for cb in range(4):
        chosen = exact_dot(local[cb * 32 : cb * 32 + 32].reshape(256, 128), hot)
        total = jnp.zeros((8, 512), f32)
        for j in range(32):
            total = jnp.where(want == j, chosen[j * 8 : j * 8 + 8], total)
        total = total * flip
        for hf in range(2):
            for h in range(2):
                at = (hf * 2 + h) * 128
                pick[cb * 2 + hf, h] = total[:, at : at + 128]

    def send_pick(de, carry):
        row, ee, _ = row_at(0, de)
        pltpu.make_async_remote_copy(
            src_ref=pick.at[ee], dst_ref=pick_in.at[e], send_sem=chain_send.at[0], recv_sem=chain_recv.at[0],
            device_id=(row, a), device_id_type=MESH,
        ).start()
        return carry

    lax.fori_loop(1, PLANE, send_pick, 0)
    pick_in[e] = pick[e]
    wait_bytes(pick_in.at[pl.ds(0, PLANE - 1)], chain_recv.at[0])
    share = jnp.sum(pick_in[...], axis=0)
    for r in range(16):
        zsum[r] = share[r // 8, r % 8 : r % 8 + 1, :]

    def send_zsum(dz, carry):
        row, _, zz = row_at(dz, 0)
        pltpu.make_async_remote_copy(
            src_ref=zsum.at[zz], dst_ref=zsum_in.at[z], send_sem=chain_send.at[1], recv_sem=chain_recv.at[1],
            device_id=(row, a), device_id_type=MESH,
        ).start()
        return carry

    lax.fori_loop(1, N_Z, send_zsum, 0)
    zsum_in[z] = zsum[z]
    wait_bytes(zsum_in.at[pl.ds(0, N_Z - 1)], chain_recv.at[1])
    row_sum = jnp.sum(zsum_in[...], axis=0)
    zrow[0] = row_sum
    zall[z] = row_sum

    def send_zrow(dz, carry):
        row, _, _ = row_at(dz, 0)
        pltpu.make_async_remote_copy(
            src_ref=zrow.at[0], dst_ref=zall.at[z], send_sem=chain_send.at[2], recv_sem=chain_recv.at[2],
            device_id=(row, a), device_id_type=MESH,
        ).start()
        return carry

    lax.fori_loop(1, N_Z, send_zrow, 0)
    wait_bytes(zall.at[pl.ds(0, N_Z - 1)], chain_recv.at[2])
    for h in range(2):
        picked[h] = jnp.concatenate([zall[h * 8 + r] for r in range(8)], axis=0)

    mine = lax.rem(e, 2) * 16 + a * 4 + lax.div(e, 2)

    def send_picked(k, carry):
        row, _, _ = row_at(0, lax.rem(k, PLANE))
        col = lax.rem(a + lax.div(k, PLANE), 4)
        pltpu.make_async_remote_copy(
            src_ref=picked, dst_ref=picked_all.at[mine], send_sem=chain_send.at[3], recv_sem=chain_recv.at[3],
            device_id=(row, col), device_id_type=MESH,
        ).start()
        return carry

    lax.fori_loop(1, 32, send_picked, 0)
    picked_all[mine] = picked[...]

    wait_bytes(first.at[pl.ds(0, 127)], recv_first)
    for hi in range(PLANE):
        first[hi * 16 : hi * 16 + 16] = butterflies(first[hi * 16 : hi * 16 + 16])
    for lo in range(N_Z):
        tiles = butterflies(jnp.stack([first[hi * 16 + lo] for hi in range(PLANE)], axis=0))
        for hi in range(PLANE):
            mixed[hi * 16 + lo] = tiles[hi]

    def send_mixed(k, carry):
        dz, de = order(k)
        row, _, _ = row_at(dz, de)
        pltpu.make_async_remote_copy(
            src_ref=mixed.at[row], dst_ref=second.at[slot, a * 4 + block],
            send_sem=send_second, recv_sem=recv_second.at[slot],
            device_id=(row, quarter), device_id_type=MESH,
        ).start()
        return carry

    away = quarter != a

    @pl.when(away)
    def _():
        pltpu.make_async_remote_copy(
            src_ref=mixed.at[p], dst_ref=second.at[slot, a * 4 + block],
            send_sem=send_second, recv_sem=recv_second.at[slot],
            device_id=(p, quarter), device_id_type=MESH,
        ).start()

    @pl.when(jnp.logical_not(away))
    def _():
        pltpu.make_async_copy(mixed.at[p], second.at[slot, a * 4 + block], recv_second.at[slot]).start()

    lax.fori_loop(1, 128, send_mixed, 0)

    wait_bytes(picked_all.at[pl.ds(0, 31)], chain_recv.at[3])
    gram = jnp.zeros((128, 128), f32)
    for hf in range(2):
        for h in range(2):
            part = picked_all[hf * 16 : hf * 16 + 16, h].reshape(128, 128)
            gram = gram + lax.dot_general(
                part, part, (((1,), (1,)), ((), ())), precision=HIGH, preferred_element_type=f32
            )
    gram = gram * f32(1.0 / 512.0)
    rows = lax.broadcasted_iota(i32, (128, 128), 0)
    cols = lax.broadcasted_iota(i32, (128, 128), 1)
    eye = (rows == cols).astype(f32)
    rest = jnp.concatenate([gram, eye], axis=1)
    for b in range(16):
        place = lax.broadcasted_iota(i32, (128 - 8 * b, 1), 0)
        for r in range(8):
            k = b * 8 + r
            pivot_row = rest[r : r + 1, :]
            pivot_row = pivot_row * (1.0 / pivot_row[:, k : k + 1])
            below = jnp.where(place > r, rest[:, k : k + 1], 0.0)
            rest = rest - below * pivot_row
        done = rest[:8]
        pivots = jnp.sum(jnp.where(eye[b * 8 : b * 8 + 8] > 0, done[:, :128], 0.0), axis=1, keepdims=True)
        factor[b * 8 : b * 8 + 8] = done[:, 128:] * lax.rsqrt(pivots)
        rest = rest[8:]

    inverse = factor[...]

    def finish(step, carry):
        at = lax.rem(z + 16 - lax.rem(3 * step, 8), 8)
        wait_bytes(second.at[at], recv_second.at[at])
        value = jnp.dot(
            inverse, second[at].reshape(128, 128), precision=HIGH, preferred_element_type=f32
        )
        result[at] = value.reshape(4, 32, 128)
        start = pl.multiple_of((a * 8 + at) * 128, 128)
        for off in range(1, 4):
            col = lax.rem(a + off, 4)
            pltpu.make_async_remote_copy(
                src_ref=result.at[at, col], dst_ref=out_ref.at[:, pl.ds(start, 128)],
                send_sem=send_out, recv_sem=recv_out,
                device_id=(p, col), device_id_type=MESH,
            ).start()
        out_ref[:, pl.ds(start, 128)] = result[at, a]
        return carry

    lax.fori_loop(0, 8, finish, 0)

    wait_bytes(out_ref.at[:, pl.ds(0, 3072)], recv_out)
    wait_bytes(local.at[pl.ds(0, 127)], send_first)
    wait_bytes(mixed.at[pl.ds(0, 127)], send_second)

    @pl.when(away)
    def _():
        wait_bytes(mixed.at[0], send_second)

    wait_bytes(result.at[pl.ds(0, 6)], send_out)
    wait_bytes(pick.at[pl.ds(0, PLANE - 1)], chain_send.at[0])
    wait_bytes(zsum.at[pl.ds(0, N_Z - 1)], chain_send.at[1])
    wait_bytes(zall.at[pl.ds(0, N_Z - 1)], chain_send.at[2])
    wait_bytes(picked_all.at[pl.ds(0, 31)], chain_send.at[3])


def shards(design_panel, sign_bits, sample_rows):
    vmem = pl.BlockSpec(memory_space=pltpu.VMEM)
    tiles = pltpu.VMEM((128, 8, 128), f32)
    dma = pltpu.SemaphoreType.DMA
    return pl.pallas_call(
        kernel,
        out_shape=jax.ShapeDtypeStruct((32, 4096), f32),
        in_specs=[vmem] * 3,
        out_specs=vmem,
        scratch_shapes=[
            tiles, tiles, tiles,
            pltpu.VMEM((8, 16, 8, 128), f32),
            pltpu.VMEM((8, 4, 32, 128), f32),
            pltpu.VMEM((8, 2, 8, 128), f32),
            pltpu.VMEM((8, 2, 8, 128), f32),
            pltpu.VMEM((16, 1, 128), f32),
            pltpu.VMEM((16, 1, 128), f32),
            pltpu.VMEM((1, 1, 128), f32),
            pltpu.VMEM((16, 1, 128), f32),
            pltpu.VMEM((2, 8, 128), f32),
            pltpu.VMEM((32, 2, 8, 128), f32),
            pltpu.VMEM((128, 128), f32),
            dma(()), dma(()), dma(()), dma((8,)), dma(()), dma(()),
            dma((4,)), dma((4,)), dma(()),
        ],
        compiler_params=pltpu.CompilerParams(has_side_effects=True, vmem_limit_bytes=32 * 2**20),
        cost_estimate=pl.CostEstimate(flops=10**9, bytes_accessed=2**20, transcendentals=0),
    )(design_panel, sign_bits.reshape(1, 4096), sample_rows.reshape(1, 512))


def solution(mesh):
    return jax.shard_map(
        shards,
        mesh=mesh,
        in_specs=(P("cols", "rows"), P("rows"), P()),
        out_specs=P("cols", "rows"),
        check_vma=False,
    )
```

time: 1440 us -> 99.3 us (0.07); the launches traced: 1410 us -> 99.1 us
  waiting for transfers between devices: 1290 us -> 0 us
  Pallas kernels: 0 us -> 95.9 us
  starting transfers between devices: 59.6 us -> 0 us
  other arithmetic: 27.3 us -> 0 us
  between operations: 15.1 us -> 0.01 us
    psum x1 -> x0, waiting for transfers between devices: 1170 us -> none  [shards(): gram_matrix = lax.psum(partial_gram, 'rows') / sample_count]
    ppermute x7 -> x0, waiting for transfers between devices: 124 us -> none  [swapped(): return lax.ppermute(value, axis, pairs)]
    pallas_call x0 -> x1, Pallas kernels: none -> 95.9 us  [shards(): pl.pallas_call(kernel, out_shape=jax.ShapeDtypeStruct((32, 4096), f32), i...]
    ppermute x7 -> x0, starting transfers between devices: 59.4 us -> none  [swapped(): return lax.ppermute(value, axis, pairs)]
    another operation x5 -> x0, other arithmetic: 23 us -> none  [the longest x3 12.5 us: shards(): lower_factor = jnp.linalg.cholesky(gram_matrix)]
  transfers between devices with their start and end apart: 9 -> 0, of which waited for: 8 -> 0; matrix products, arithmetic and copies ran while one was open for 2% -> 0% of each run, Pallas kernels for 0% -> 0%
where the time goes in v1:
time: 99.3 us; the launch traced here: 99.1 us
  Pallas kernels  95.9 us (97%)
  local copies, waits for them, and re-layouts  3.23 us (3%)
    pallas_call x1, Pallas kernels, shards(): pl.pallas_call(kernel, out_shape=jax.ShapeDtypeStruct((32, 4096), f32), i...  95.9 us
    unnamed x7, local copies, waits for them, and re-layouts  3.23 us

profile of v1, /device:TPU:1, one launch (start us, length us, event | category | flops | bytes accessed | tf_op | source)
XLA Modules:
  0.0 99.1 jit_solution(9589396161685162544)
XLA Ops:
  0.0 0.0 copy-start.2
  0.0 0.7 copy-done.2
  0.7 0.0 copy-start
  0.7 1.0 %copy-done = f32[32,4096]{1,0:T(8,128)S(1)} copy-done((f32[32,4096]{1,0:T(8,128)S(1)}, f32[32,4096]{1,0:T(8,128)}, u32[]{:S(2)}) %copy-start) | copy-done | bytes 524312
  1.7 0.0 copy-start.1
  1.7 0.7 copy-done.1
  2.4 95.9 %shard_map.37 = f32[32,4096]{1,0:T(8,128)S(1)} custom-call(f32[32,4096]{1,0:T(8,128)S(1)} %copy-done, s32[1,4096]{1,0:T(1,128)S(1)} %bitcast.2, s32[1,512]{1,0:T(1,128)S(1)} %bitcast.3), custom_call_target="tpu_custom_call" | custom-call | flops 1000000000 | bytes 1048576 | tf_op jit(solution)/shard_map/pallas_call | solution.py:284
  98.3 0.8 copy.5
Async XLA Ops:
  0.0 0.7 copy-start.2
  0.7 1.0 %copy-start = (f32[32,4096]{1,0:T(8,128)S(1)}, f32[32,4096]{1,0:T(8,128)}, u32[]{:S(2)}) copy-start(f32[32,4096]{1,0:T(8,128)} %x_ref.1) | copy-start | bytes 1572868
  1.7 0.7 copy-start.1

commit v2 on v1

v2 whole, which is shorter than its diff:
```python
import functools
import math

import jax
import jax.numpy as jnp
from jax import lax
from jax.experimental import pallas as pl
from jax.experimental.pallas import tpu as pltpu
from jax.sharding import PartitionSpec as P

MESH = pl.DeviceIdType.MESH
f32, bf16, i32 = jnp.float32, jnp.bfloat16, jnp.int32
HIGH = lax.Precision.HIGHEST
N_X, N_Z = 4, 16
PLANE = 8
CUT_A, CUT_B = 5, 10
EARLY = False


def parity(value, bits):
    shift = bits // 2
    while shift:
        value = value ^ (value >> shift)
        shift //= 2
    return value & 1


def sylvester(n):
    rows = lax.broadcasted_iota(i32, (n, n), 0)
    cols = lax.broadcasted_iota(i32, (n, n), 1)
    return (1 - 2 * parity(rows & cols, 8)).astype(f32).astype(bf16)


def parts(value):
    high = value.astype(bf16)
    rest = value - high.astype(f32)
    middle = rest.astype(bf16)
    low = (rest - middle.astype(f32)).astype(bf16)
    return high, middle, low


def exact_dot(value, table):
    high, middle, low = parts(value)
    dot = functools.partial(jnp.dot, preferred_element_type=f32)
    return dot(low, table) + dot(middle, table) + dot(high, table)


def butterflies(tiles):
    n = tiles.shape[0]
    half = 1
    while half < n:
        pairs = tiles.reshape(n // (2 * half), 2, half, 8, 128)
        a, b = pairs[:, 0], pairs[:, 1]
        tiles = jnp.stack([a + b, a - b], axis=1).reshape(n, 8, 128)
        half *= 2
    return tiles


def wait_bytes(ref, sem):
    pltpu.make_async_copy(ref, ref, sem).wait()


def kernel(
    x_hbm, sign_hbm, sample_hbm, out_ref,
    x_ref, sign_ref, sample_ref,
    local, first, mixed, second, result,
    pick, pick_in, zsum, zsum_in, zrow, zall, picked, picked_all, factor,
    load_sem, go_sem,
    send_first, recv_first, send_second, recv_second, send_out, recv_out,
    chain_send, chain_recv,
):
    loads = [
        pltpu.make_async_copy(source, target, load_sem.at[n])
        for n, (source, target) in enumerate(
            ((x_hbm, x_ref), (sign_hbm, sign_ref), (sample_hbm, sample_ref))
        )
    ]
    for load in loads:
        load.start()

    p = lax.axis_index("rows")
    a = lax.axis_index("cols")
    z = lax.rem(p, N_Z)
    x = lax.rem(lax.div(p, N_Z), N_X)
    y = lax.div(p, N_Z * N_X)
    e = y * N_X + x
    quarter = lax.rem(x, 2) * 2 + lax.div(z, 8)
    slot = lax.rem(z, 8)
    block = y * 2 + lax.div(x, 2)
    plane = []
    for de in range(PLANE):
        plane.append(lax.rem(y + de // N_X, 2) * N_X + lax.rem(x + de % N_X, N_X))
    base = [at * N_Z for at in plane]
    col = [a] + [lax.rem(a + k, 4) for k in range(1, 4)]

    def along(dz):
        return lax.rem(z + dz, N_Z)

    def far_first(i):
        return 8 + lax.div(i + 1, 2) * (1 - 2 * lax.rem(i, 2))

    def even(i):
        middle = lax.div(i + 1, 2)
        return lax.rem(8 + middle * (2 * lax.rem(i, 2) - 1), 8)

    def remote(source, target, send, recv, row, column):
        pltpu.make_async_remote_copy(
            src_ref=source, dst_ref=target, send_sem=send, recv_sem=recv,
            device_id=(row, column), device_id_type=MESH,
        ).start()

    def signal(sem, row, column):
        pl.semaphore_signal(sem, inc=1, device_id=(row, column), device_id_type=MESH)

    barrier = pltpu.get_barrier_semaphore()

    def greet(i, carry):
        signal(barrier, base[0] + along(far_first(i)), a)
        return carry

    lax.fori_loop(0, N_Z - 1, greet, 0, unroll=True)
    for de in range(1, PLANE):
        signal(barrier, base[de] + z, a)
    for k in range(1, 4):
        signal(barrier, p, col[k])

    for load in loads:
        load.wait()
    scale = f32(1.0 / math.sqrt(524288.0))
    signs = (2 * sign_ref[...] - 1).astype(f32) * scale
    table = sylvester(128)
    for cb in range(4):
        flipped = x_ref[cb * 8 : cb * 8 + 8, :] * signs
        tiles = jnp.concatenate([flipped[:, j * 128 : j * 128 + 128] for j in range(32)], axis=0)
        tiles = exact_dot(tiles, table).reshape(32, 8, 128)
        local[cb * 32 : cb * 32 + 32] = butterflies(tiles)

    samples = sample_ref[...]
    hot = (lax.broadcasted_iota(i32, (128, 512), 0) == lax.rem(samples, 128)).astype(f32).astype(bf16)
    want = jnp.broadcast_to(lax.rem(lax.div(samples, 128), 32), (8, 512))
    flip = (1 - 2 * parity(lax.div(samples, 4096) & p, 8)).astype(f32)
    for cb in range(4):
        chosen = exact_dot(local[cb * 32 : cb * 32 + 32].reshape(256, 128), hot)
        total = jnp.zeros((8, 512), f32)
        for j in range(32):
            total = jnp.where(want == j, chosen[j * 8 : j * 8 + 8], total)
        total = total * flip
        for hf in range(2):
            for h in range(2):
                at = (hf * 2 + h) * 128
                pick[cb * 2 + hf, h] = total[:, at : at + 128]

    pl.semaphore_wait(barrier, N_Z - 1 + PLANE - 1 + 3)

    def greet_again(i, carry):
        signal(go_sem, base[0] + along(far_first(i)), a)
        return carry

    lax.fori_loop(0, N_Z - 1, greet_again, 0, unroll=True)

    for de in range(1, PLANE):
        remote(pick.at[plane[de]], pick_in.at[e], chain_send.at[0], chain_recv.at[0], base[de] + z, a)

    def send_tile(row):
        remote(local.at[row], first.at[p], send_first, recv_first, row, a)

    def send_line(i, carry):
        send_tile(base[0] + along(far_first(i)))
        return carry

    def send_planes(i, carry):
        zz = along(far_first(i))
        for de in range(1, PLANE):
            send_tile(base[de] + zz)
        return carry

    lax.fori_loop(0, N_Z - 1, send_line, 0, unroll=True)
    pl.semaphore_wait(go_sem, N_Z - 1)
    lax.fori_loop(0, CUT_A, send_planes, 0)
    first[p] = local[p]
    pick_in[e] = pick[e]

    wait_bytes(pick_in.at[pl.ds(0, PLANE - 1)], chain_recv.at[0])
    share = jnp.sum(pick_in[...], axis=0)
    for r in range(16):
        zsum[r] = share[r // 8, r % 8 : r % 8 + 1, :]

    def send_zsum(i, carry):
        zz = along(far_first(i))
        remote(zsum.at[zz], zsum_in.at[z], chain_send.at[1], chain_recv.at[1], base[0] + zz, a)
        return carry

    lax.fori_loop(0, N_Z - 1, send_zsum, 0, unroll=True)
    zsum_in[z] = zsum[z]
    lax.fori_loop(CUT_A, CUT_B, send_planes, 0)
    wait_bytes(zsum_in.at[pl.ds(0, N_Z - 1)], chain_recv.at[1])
    row_sum = jnp.sum(zsum_in[...], axis=0)
    zrow[0] = row_sum
    zall[z] = row_sum

    def send_zrow(i, carry):
        remote(zrow.at[0], zall.at[z], chain_send.at[2], chain_recv.at[2], base[0] + along(far_first(i)), a)
        return carry

    lax.fori_loop(0, N_Z - 1, send_zrow, 0, unroll=True)
    lax.fori_loop(CUT_B, N_Z - 1, send_planes, 0)
    for de in range(1, PLANE):
        send_tile(base[de] + z)

    mine = lax.rem(e, 2) * 16 + a * 4 + lax.div(e, 2)

    def share_picked():
        wait_bytes(zall.at[pl.ds(0, N_Z - 1)], chain_recv.at[2])
        for h in range(2):
            picked[h] = jnp.concatenate([zall[h * 8 + r] for r in range(8)], axis=0)
        for de in range(PLANE):
            for k in range(4):
                if de or k:
                    remote(
                        picked, picked_all.at[mine], chain_send.at[3], chain_recv.at[3],
                        base[de] + z, col[k],
                    )
        picked_all[mine] = picked[...]

    if EARLY:
        share_picked()

    wait_bytes(first.at[pl.ds(0, 127)], recv_first)
    for hi in range(PLANE):
        first[hi * 16 : hi * 16 + 16] = butterflies(first[hi * 16 : hi * 16 + 16])
    target = second.at[slot, a * 4 + block]
    landed = recv_second.at[slot]
    away = quarter != a

    def mix_and_send(zz, own):
        tiles = butterflies(jnp.stack([first[hi * 16 + zz] for hi in range(PLANE)], axis=0))
        for hi in range(PLANE):
            mixed[hi * 16 + zz] = tiles[hi]
        for de in range(1 if own else 0, PLANE):
            remote(mixed.at[base[de] + zz], target, send_second, landed, base[de] + zz, quarter)

    def send_mixed(i, carry):
        mix_and_send(along(even(i)), False)
        mix_and_send(along(even(i) + 8), False)
        return carry

    mix_and_send(along(8), False)
    mix_and_send(z, True)

    @pl.when(away)
    def _():
        remote(mixed.at[p], target, send_second, landed, p, quarter)

    @pl.when(jnp.logical_not(away))
    def _():
        pltpu.make_async_copy(mixed.at[p], target, landed).start()

    lax.fori_loop(1, 8, send_mixed, 0)
    if not EARLY:
        share_picked()

    wait_bytes(picked_all.at[pl.ds(0, 31)], chain_recv.at[3])
    gram = jnp.zeros((128, 128), f32)
    for hf in range(2):
        for h in range(2):
            part = picked_all[hf * 16 : hf * 16 + 16, h].reshape(128, 128)
            gram = gram + lax.dot_general(
                part, part, (((1,), (1,)), ((), ())), precision=HIGH, preferred_element_type=f32
            )
    gram = gram * f32(1.0 / 512.0)
    rows = lax.broadcasted_iota(i32, (128, 128), 0)
    cols = lax.broadcasted_iota(i32, (128, 128), 1)
    eye = (rows == cols).astype(f32)
    rest = jnp.concatenate([gram, eye], axis=1)
    for b in range(16):
        place = lax.broadcasted_iota(i32, (128 - 8 * b, 1), 0)
        for r in range(8):
            k = b * 8 + r
            pivot_row = rest[r : r + 1, :]
            pivot_row = pivot_row * (1.0 / pivot_row[:, k : k + 1])
            below = jnp.where(place > r, rest[:, k : k + 1], 0.0)
            rest = rest - below * pivot_row
        done = rest[:8]
        pivots = jnp.sum(jnp.where(eye[b * 8 : b * 8 + 8] > 0, done[:, :128], 0.0), axis=1, keepdims=True)
        factor[b * 8 : b * 8 + 8] = done[:, 128:] * lax.rsqrt(pivots)
        rest = rest[8:]

    inverse = factor[...]

    def finish(step, carry):
        at = lax.rem(z + 8 - even(step), 8)
        wait_bytes(second.at[at], recv_second.at[at])
        value = jnp.dot(
            inverse, second[at].reshape(128, 128), precision=HIGH, preferred_element_type=f32
        )
        result[at] = value.reshape(4, 32, 128)
        start = pl.multiple_of((a * 8 + at) * 128, 128)
        there = out_ref.at[:, pl.ds(start, 128)]
        for k in range(1, 4):
            remote(result.at[at, col[k]], there, send_out, recv_out, p, col[k])
        pltpu.make_async_copy(result.at[at, a], there, recv_out).start()
        return carry

    lax.fori_loop(0, 8, finish, 0)

    wait_bytes(out_ref, recv_out)
    wait_bytes(local.at[pl.ds(0, 127)], send_first)
    wait_bytes(mixed.at[pl.ds(0, 127)], send_second)

    @pl.when(away)
    def _():
        wait_bytes(mixed.at[0], send_second)

    wait_bytes(result.at[pl.ds(0, 6)], send_out)
    wait_bytes(pick.at[pl.ds(0, PLANE - 1)], chain_send.at[0])
    wait_bytes(zsum.at[pl.ds(0, N_Z - 1)], chain_send.at[1])
    wait_bytes(zall.at[pl.ds(0, N_Z - 1)], chain_send.at[2])
    wait_bytes(picked_all.at[pl.ds(0, 31)], chain_send.at[3])


def shards(design_panel, sign_bits, sample_rows):
    anywhere = pl.BlockSpec(memory_space=pl.ANY)
    tiles = pltpu.VMEM((128, 8, 128), f32)
    dma = pltpu.SemaphoreType.DMA
    return pl.pallas_call(
        kernel,
        out_shape=jax.ShapeDtypeStruct((32, 4096), f32),
        in_specs=[anywhere] * 3,
        out_specs=anywhere,
        scratch_shapes=[
            pltpu.VMEM((32, 4096), f32),
            pltpu.VMEM((1, 4096), i32),
            pltpu.VMEM((1, 512), i32),
            tiles, tiles, tiles,
            pltpu.VMEM((8, 16, 8, 128), f32),
            pltpu.VMEM((8, 4, 32, 128), f32),
            pltpu.VMEM((8, 2, 8, 128), f32),
            pltpu.VMEM((8, 2, 8, 128), f32),
            pltpu.VMEM((16, 1, 128), f32),
            pltpu.VMEM((16, 1, 128), f32),
            pltpu.VMEM((1, 1, 128), f32),
            pltpu.VMEM((16, 1, 128), f32),
            pltpu.VMEM((2, 8, 128), f32),
            pltpu.VMEM((32, 2, 8, 128), f32),
            pltpu.VMEM((128, 128), f32),
            dma((3,)), pltpu.SemaphoreType.REGULAR,
            dma(()), dma(()), dma(()), dma((8,)), dma(()), dma(()),
            dma((4,)), dma((4,)),
        ],
        compiler_params=pltpu.CompilerParams(
            collective_id=0, has_side_effects=True, vmem_limit_bytes=32 * 2**20
        ),
        cost_estimate=pl.CostEstimate(flops=10**9, bytes_accessed=2**20, transcendentals=0),
    )(design_panel, sign_bits.reshape(1, 4096), sample_rows.reshape(1, 512))


def solution(mesh):
    return jax.shard_map(
        shards,
        mesh=mesh,
        in_specs=(P("cols", "rows"), P("rows"), P()),
        out_specs=P("cols", "rows"),
        check_vma=False,
    )
```

time: 99.3 us -> 78.4 us (0.79)
  Pallas kernels: 95.9 us -> 75 us
    pallas_call x1, Pallas kernels: 95.9 us -> 75 us  [shards(): pl.pallas_call(kernel, out_shape=jax.ShapeDtypeStruct((32, 4096), f32), i...]
where the time goes in v2:
time: 78.4 us; the launch traced here: 78.2 us
  Pallas kernels  75 us (96%)
  local copies, waits for them, and re-layouts  3.23 us (4%)
    pallas_call x1, Pallas kernels, shards(): pl.pallas_call(kernel, out_shape=jax.ShapeDtypeStruct((32, 4096), f32), i...  75 us
    unnamed x7, local copies, waits for them, and re-layouts  3.23 us

profile of v2, /device:TPU:1, one launch (start us, length us, event | category | flops | bytes accessed | tf_op | source)
XLA Modules:
  0.0 78.2 jit_solution(10382926719255539193)
XLA Ops:
  0.0 0.0 copy-start.2
  0.0 0.7 copy-done.2
  0.7 0.0 copy-start
  0.7 1.0 %copy-done = f32[32,4096]{1,0:T(8,128)S(1)} copy-done((f32[32,4096]{1,0:T(8,128)S(1)}, f32[32,4096]{1,0:T(8,128)}, u32[]{:S(2)}) %copy-start) | copy-done | bytes 524312
  1.7 0.0 copy-start.1
  1.7 0.7 copy-done.1
  2.4 75.0 %shard_map.37 = f32[32,4096]{1,0:T(8,128)S(1)} custom-call(f32[32,4096]{1,0:T(8,128)S(1)} %copy-done, s32[1,4096]{1,0:T(1,128)S(1)} %bitcast.2, s32[1,512]{1,0:T(1,128)S(1)} %bitcast.3), custom_call_target="tpu_custom_call" | custom-call | flops 1000000000 | bytes 1048576 | tf_op jit(solution)/shard_map/pallas_call | solution.py:325
  77.4 0.8 %copy.5 = f32[32,4096]{1,0:T(8,128)} copy(f32[32,4096]{1,0:T(8,128)S(1)} %shard_map.37) | data formatting | bytes 1048576
Async XLA Ops:
  0.0 0.7 copy-start.2
  0.7 1.0 %copy-start = (f32[32,4096]{1,0:T(8,128)S(1)}, f32[32,4096]{1,0:T(8,128)}, u32[]{:S(2)}) copy-start(f32[32,4096]{1,0:T(8,128)} %x_hbm.1) | copy-start | bytes 1572868
  1.7 0.7 copy-start.1

commit v3 on v2

--- a/solution.py
+++ b/solution.py
@@ -13,8 +13,10 @@
 HIGH = lax.Precision.HIGHEST
 N_X, N_Z = 4, 16
 PLANE = 8
-CUT_A, CUT_B = 5, 10
-EARLY = False
+HALVES = 2
+PARTS = tuple(slice(8 // HALVES * n, 8 // HALVES * (n + 1)) for n in range(HALVES))
+FAR = (6, 5, 7, 2, 4, 1, 3, 0)
+NEAR = (0, 1, 3)
 
 
 def parity(value, bits):
@@ -46,12 +48,12 @@
 
 
 def butterflies(tiles):
-    n = tiles.shape[0]
+    n, rows, _ = tiles.shape
     half = 1
     while half < n:
-        pairs = tiles.reshape(n // (2 * half), 2, half, 8, 128)
+        pairs = tiles.reshape(n // (2 * half), 2, half, rows, 128)
         a, b = pairs[:, 0], pairs[:, 1]
-        tiles = jnp.stack([a + b, a - b], axis=1).reshape(n, 8, 128)
+        tiles = jnp.stack([a + b, a - b], axis=1).reshape(n, rows, 128)
         half *= 2
     return tiles
 
@@ -115,7 +117,9 @@
     barrier = pltpu.get_barrier_semaphore()
 
     def greet(i, carry):
-        signal(barrier, base[0] + along(far_first(i)), a)
+        zz = along(far_first(i))
+        for de in NEAR:
+            signal(barrier, base[de] + zz, a)
         return carry
 
     lax.fori_loop(0, N_Z - 1, greet, 0, unroll=True)
@@ -150,7 +154,7 @@
                 at = (hf * 2 + h) * 128
                 pick[cb * 2 + hf, h] = total[:, at : at + 128]
 
-    pl.semaphore_wait(barrier, N_Z - 1 + PLANE - 1 + 3)
+    pl.semaphore_wait(barrier, (N_Z - 1) * len(NEAR) + PLANE - 1 + 3)
 
     def greet_again(i, carry):
         signal(go_sem, base[0] + along(far_first(i)), a)
@@ -161,24 +165,27 @@
     for de in range(1, PLANE):
         remote(pick.at[plane[de]], pick_in.at[e], chain_send.at[0], chain_recv.at[0], base[de] + z, a)
 
-    def send_tile(row):
-        remote(local.at[row], first.at[p], send_first, recv_first, row, a)
-
-    def send_line(i, carry):
-        send_tile(base[0] + along(far_first(i)))
-        return carry
-
-    def send_planes(i, carry):
-        zz = along(far_first(i))
-        for de in range(1, PLANE):
-            send_tile(base[de] + zz)
-        return carry
-
-    lax.fori_loop(0, N_Z - 1, send_line, 0, unroll=True)
+    def send_tile(row, n):
+        remote(local.at[row, PARTS[n]], first.at[p, PARTS[n]], send_first, recv_first.at[n], row, a)
+
+    def send_tiles(n, some):
+        def send_plane(i, carry):
+            zz = along(far_first(i))
+            for de in some:
+                send_tile(base[de] + zz, n)
+            return carry
+
+        return send_plane
+
+    others = tuple(de for de in FAR if de not in NEAR)
+    lax.fori_loop(0, N_Z - 1, send_tiles(0, NEAR), 0, unroll=3)
+    for de in FAR[:-1]:
+        send_tile(base[de] + z, 0)
     pl.semaphore_wait(go_sem, N_Z - 1)
-    lax.fori_loop(0, CUT_A, send_planes, 0)
     first[p] = local[p]
     pick_in[e] = pick[e]
+
+    lax.fori_loop(0, N_Z - 1, send_tiles(0, others), 0)
 
     wait_bytes(pick_in.at[pl.ds(0, PLANE - 1)], chain_recv.at[0])
     share = jnp.sum(pick_in[...], axis=0)
@@ -192,7 +199,7 @@
 
     lax.fori_loop(0, N_Z - 1, send_zsum, 0, unroll=True)
     zsum_in[z] = zsum[z]
-    lax.fori_loop(CUT_A, CUT_B, send_planes, 0)
+    lax.fori_loop(0, 8, send_tiles(1, FAR), 0)
     wait_bytes(zsum_in.at[pl.ds(0, N_Z - 1)], chain_recv.at[1])
     row_sum = jnp.sum(zsum_in[...], axis=0)
     zrow[0] = row_sum
@@ -203,9 +210,9 @@
         return carry
 
     lax.fori_loop(0, N_Z - 1, send_zrow, 0, unroll=True)
-    lax.fori_loop(CUT_B, N_Z - 1, send_planes, 0)
-    for de in range(1, PLANE):
-        send_tile(base[de] + z)
+    lax.fori_loop(8, N_Z - 1, send_tiles(1, FAR), 0)
+    for de in FAR[:-1]:
+        send_tile(base[de] + z, 1)
 
     mine = lax.rem(e, 2) * 16 + a * 4 + lax.div(e, 2)
 
@@ -222,42 +229,43 @@
                     )
         picked_all[mine] = picked[...]
 
-    if EARLY:
-        share_picked()
-
-    wait_bytes(first.at[pl.ds(0, 127)], recv_first)
-    for hi in range(PLANE):
-        first[hi * 16 : hi * 16 + 16] = butterflies(first[hi * 16 : hi * 16 + 16])
-    target = second.at[slot, a * 4 + block]
     landed = recv_second.at[slot]
     away = quarter != a
 
-    def mix_and_send(zz, own):
-        tiles = butterflies(jnp.stack([first[hi * 16 + zz] for hi in range(PLANE)], axis=0))
+    def mix_and_send(n, zz, own):
+        part = PARTS[n]
+        target = second.at[slot, a * 4 + block, part]
+        tiles = butterflies(jnp.stack([first[hi * 16 + zz, part] for hi in range(PLANE)], axis=0))
         for hi in range(PLANE):
-            mixed[hi * 16 + zz] = tiles[hi]
-        for de in range(1 if own else 0, PLANE):
-            remote(mixed.at[base[de] + zz], target, send_second, landed, base[de] + zz, quarter)
-
-    def send_mixed(i, carry):
-        mix_and_send(along(even(i)), False)
-        mix_and_send(along(even(i) + 8), False)
-        return carry
-
-    mix_and_send(along(8), False)
-    mix_and_send(z, True)
-
-    @pl.when(away)
-    def _():
-        remote(mixed.at[p], target, send_second, landed, p, quarter)
-
-    @pl.when(jnp.logical_not(away))
-    def _():
-        pltpu.make_async_copy(mixed.at[p], target, landed).start()
-
-    lax.fori_loop(1, 8, send_mixed, 0)
-    if not EARLY:
-        share_picked()
+            mixed[hi * 16 + zz, part] = tiles[hi]
+        for de in FAR[: PLANE - own]:
+            remote(mixed.at[base[de] + zz, part], target, send_second, landed, base[de] + zz, quarter)
+        if own:
+
+            @pl.when(away)
+            def _():
+                remote(mixed.at[p, part], target, send_second, landed, p, quarter)
+
+            @pl.when(jnp.logical_not(away))
+            def _():
+                pltpu.make_async_copy(mixed.at[p, part], target, landed).start()
+
+    for n in range(HALVES):
+        part = PARTS[n]
+        wait_bytes(first.at[pl.ds(0, 127), part], recv_first.at[n])
+        for hi in range(PLANE):
+            first[hi * 16 : hi * 16 + 16, part] = butterflies(first[hi * 16 : hi * 16 + 16, part])
+
+        def send_mixed(i, carry):
+            mix_and_send(n, along(even(i)), False)
+            mix_and_send(n, along(even(i) + 8), False)
+            return carry
+
+        mix_and_send(n, along(8), False)
+        mix_and_send(n, z, True)
+        lax.fori_loop(1, 8, send_mixed, 0)
+        if n == 0:
+            share_picked()
 
     wait_bytes(picked_all.at[pl.ds(0, 31)], chain_recv.at[3])
     gram = jnp.zeros((128, 128), f32)
@@ -344,7 +352,7 @@
             pltpu.VMEM((32, 2, 8, 128), f32),
             pltpu.VMEM((128, 128), f32),
             dma((3,)), pltpu.SemaphoreType.REGULAR,
-            dma(()), dma(()), dma(()), dma((8,)), dma(()), dma(()),
+            dma(()), dma((HALVES,)), dma(()), dma((8,)), dma(()), dma(()),
             dma((4,)), dma((4,)),
         ],
         compiler_params=pltpu.CompilerParams(

time: 78.4 us -> 76.3 us (0.973)
  Pallas kernels: 75 us -> 72.8 us
    pallas_call x1, Pallas kernels: 75 us -> 72.8 us  [shards(): pl.pallas_call(kernel, out_shape=jax.ShapeDtypeStruct((32, 4096), f32), i...]
where the time goes in v3:
time: 76.3 us; the launch traced here: 76 us
  Pallas kernels  72.8 us (95%)
  local copies, waits for them, and re-layouts  3.23 us (4%)
    pallas_call x1, Pallas kernels, shards(): pl.pallas_call(kernel, out_shape=jax.ShapeDtypeStruct((32, 4096), f32), i...  72.8 us
    unnamed x7, local copies, waits for them, and re-layouts  3.23 us

profile of v3, /device:TPU:1, one launch (start us, length us, event | category | flops | bytes accessed | tf_op | source)
XLA Modules:
  0.0 76.0 jit_solution(204570377158704009)
XLA Ops:
  0.0 0.0 copy-start.2
  0.0 0.7 copy-done.2
  0.7 0.0 copy-start
  0.7 1.0 %copy-done = f32[32,4096]{1,0:T(8,128)S(1)} copy-done((f32[32,4096]{1,0:T(8,128)S(1)}, f32[32,4096]{1,0:T(8,128)}, u32[]{:S(2)}) %copy-start) | copy-done | bytes 524312
  1.7 0.0 copy-start.1
  1.7 0.7 copy-done.1
  2.4 72.8 %shard_map.37 = f32[32,4096]{1,0:T(8,128)S(1)} custom-call(f32[32,4096]{1,0:T(8,128)S(1)} %copy-done, s32[1,4096]{1,0:T(1,128)S(1)} %bitcast.2, s32[1,512]{1,0:T(1,128)S(1)} %bitcast.3), custom_call_target="tpu_custom_call" | custom-call | flops 1000000000 | bytes 1048576 | tf_op jit(solution)/shard_map/pallas_call | solution.py:333
  75.2 0.8 %copy.5 = f32[32,4096]{1,0:T(8,128)} copy(f32[32,4096]{1,0:T(8,128)S(1)} %shard_map.37) | data formatting | bytes 1048576
Async XLA Ops:
  0.0 0.7 copy-start.2
  0.7 1.0 %copy-start = (f32[32,4096]{1,0:T(8,128)S(1)}, f32[32,4096]{1,0:T(8,128)}, u32[]{:S(2)}) copy-start(f32[32,4096]{1,0:T(8,128)} %x_hbm.1) | copy-start | bytes 1572868
  1.7 0.7 copy-start.1

commit v4 on v3

--- a/solution.py
+++ b/solution.py
@@ -17,6 +17,8 @@
 PARTS = tuple(slice(8 // HALVES * n, 8 // HALVES * (n + 1)) for n in range(HALVES))
 FAR = (6, 5, 7, 2, 4, 1, 3, 0)
 NEAR = (0, 1, 3)
+CLOSE = (4, 12, 3, 13, 2, 14, 1, 15)
+DISTANT = (8, 7, 9, 6, 10, 5, 11)
 
 
 def parity(value, bits):
@@ -116,13 +118,9 @@
 
     barrier = pltpu.get_barrier_semaphore()
 
-    def greet(i, carry):
-        zz = along(far_first(i))
+    for dz in CLOSE:
         for de in NEAR:
-            signal(barrier, base[de] + zz, a)
-        return carry
-
-    lax.fori_loop(0, N_Z - 1, greet, 0, unroll=True)
+            signal(barrier, base[de] + along(dz), a)
     for de in range(1, PLANE):
         signal(barrier, base[de] + z, a)
     for k in range(1, 4):
@@ -154,13 +152,13 @@
                 at = (hf * 2 + h) * 128
                 pick[cb * 2 + hf, h] = total[:, at : at + 128]
 
-    pl.semaphore_wait(barrier, (N_Z - 1) * len(NEAR) + PLANE - 1 + 3)
-
-    def greet_again(i, carry):
-        signal(go_sem, base[0] + along(far_first(i)), a)
-        return carry
-
-    lax.fori_loop(0, N_Z - 1, greet_again, 0, unroll=True)
+    pl.semaphore_wait(barrier, len(CLOSE) * len(NEAR) + PLANE - 1 + 3)
+
+    def tell(sem):
+        for dz in CLOSE:
+            signal(sem, base[0] + along(dz), a)
+
+    tell(go_sem.at[0])
 
     for de in range(1, PLANE):
         remote(pick.at[plane[de]], pick_in.at[e], chain_send.at[0], chain_recv.at[0], base[de] + z, a)
@@ -168,24 +166,26 @@
     def send_tile(row, n):
         remote(local.at[row, PARTS[n]], first.at[p, PARTS[n]], send_first, recv_first.at[n], row, a)
 
-    def send_tiles(n, some):
-        def send_plane(i, carry):
-            zz = along(far_first(i))
+    def send_tiles(n, steps, some):
+        for dz in steps:
+            zz = along(dz)
             for de in some:
                 send_tile(base[de] + zz, n)
-            return carry
-
-        return send_plane
 
     others = tuple(de for de in FAR if de not in NEAR)
-    lax.fori_loop(0, N_Z - 1, send_tiles(0, NEAR), 0, unroll=3)
+    send_tiles(0, CLOSE, NEAR)
     for de in FAR[:-1]:
         send_tile(base[de] + z, 0)
-    pl.semaphore_wait(go_sem, N_Z - 1)
+    send_tiles(1, CLOSE, NEAR)
+    pl.semaphore_wait(go_sem.at[0], len(CLOSE))
+    tell(go_sem.at[1])
+    send_tiles(0, CLOSE, others)
+    send_tiles(0, DISTANT, NEAR)
+    pl.semaphore_wait(go_sem.at[1], len(CLOSE))
+    send_tiles(0, DISTANT, others)
     first[p] = local[p]
     pick_in[e] = pick[e]
 
-    lax.fori_loop(0, N_Z - 1, send_tiles(0, others), 0)
 
     wait_bytes(pick_in.at[pl.ds(0, PLANE - 1)], chain_recv.at[0])
     share = jnp.sum(pick_in[...], axis=0)
@@ -199,7 +199,7 @@
 
     lax.fori_loop(0, N_Z - 1, send_zsum, 0, unroll=True)
     zsum_in[z] = zsum[z]
-    lax.fori_loop(0, 8, send_tiles(1, FAR), 0)
+    send_tiles(1, DISTANT, FAR)
     wait_bytes(zsum_in.at[pl.ds(0, N_Z - 1)], chain_recv.at[1])
     row_sum = jnp.sum(zsum_in[...], axis=0)
     zrow[0] = row_sum
@@ -210,7 +210,7 @@
         return carry
 
     lax.fori_loop(0, N_Z - 1, send_zrow, 0, unroll=True)
-    lax.fori_loop(8, N_Z - 1, send_tiles(1, FAR), 0)
+    send_tiles(1, CLOSE, others)
     for de in FAR[:-1]:
         send_tile(base[de] + z, 1)
 
@@ -351,7 +351,7 @@
             pltpu.VMEM((2, 8, 128), f32),
             pltpu.VMEM((32, 2, 8, 128), f32),
             pltpu.VMEM((128, 128), f32),
-            dma((3,)), pltpu.SemaphoreType.REGULAR,
+            dma((3,)), pltpu.SemaphoreType.REGULAR((2,)),
             dma(()), dma((HALVES,)), dma(()), dma((8,)), dma(()), dma(()),
             dma((4,)), dma((4,)),
         ],

time: 76.3 us -> 74.1 us (0.971)
  Pallas kernels: 72.8 us -> 70.7 us
    pallas_call x1, Pallas kernels: 72.8 us -> 70.7 us  [shards(): pl.pallas_call(kernel, out_shape=jax.ShapeDtypeStruct((32, 4096), f32), i...]
where the time goes in v4:
time: 74.1 us; the launch traced here: 73.9 us
  Pallas kernels  70.7 us (95%)
  local copies, waits for them, and re-layouts  3.23 us (4%)
    pallas_call x1, Pallas kernels, shards(): pl.pallas_call(kernel, out_shape=jax.ShapeDtypeStruct((32, 4096), f32), i...  70.7 us
    unnamed x7, local copies, waits for them, and re-layouts  3.23 us

profile of v4, /device:TPU:1, one launch (start us, length us, event | category | flops | bytes accessed | tf_op | source)
XLA Modules:
  0.0 73.9 jit_solution(3343953903201324609)
XLA Ops:
  0.0 0.0 copy-start.2
  0.0 0.7 copy-done.2
  0.7 0.0 copy-start
  0.7 1.0 %copy-done = f32[32,4096]{1,0:T(8,128)S(1)} copy-done((f32[32,4096]{1,0:T(8,128)S(1)}, f32[32,4096]{1,0:T(8,128)}, u32[]{:S(2)}) %copy-start) | copy-done | bytes 524312
  1.7 0.0 copy-start.1
  1.7 0.7 copy-done.1
  2.4 70.7 %shard_map.37 = f32[32,4096]{1,0:T(8,128)S(1)} custom-call(f32[32,4096]{1,0:T(8,128)S(1)} %copy-done, s32[1,4096]{1,0:T(1,128)S(1)} %bitcast.2, s32[1,512]{1,0:T(1,128)S(1)} %bitcast.3), custom_call_target="tpu_custom_call" | custom-call | flops 1000000000 | bytes 1048576 | tf_op jit(solution)/shard_map/pallas_call | solution.py:333
  73.1 0.8 %copy.5 = f32[32,4096]{1,0:T(8,128)} copy(f32[32,4096]{1,0:T(8,128)S(1)} %shard_map.37) | data formatting | bytes 1048576
Async XLA Ops:
  0.0 0.7 copy-start.2
  0.7 1.0 %copy-start = (f32[32,4096]{1,0:T(8,128)S(1)}, f32[32,4096]{1,0:T(8,128)}, u32[]{:S(2)}) copy-start(f32[32,4096]{1,0:T(8,128)} %x_hbm.1) | copy-start | bytes 1572868
  1.7 0.7 copy-start.1

commit v5 on v4

--- a/solution.py
+++ b/solution.py
@@ -79,9 +79,6 @@
             ((x_hbm, x_ref), (sign_hbm, sign_ref), (sample_hbm, sample_ref))
         )
     ]
-    for load in loads:
-        load.start()
-
     p = lax.axis_index("rows")
     a = lax.axis_index("cols")
     z = lax.rem(p, N_Z)
@@ -126,6 +123,8 @@
     for k in range(1, 4):
         signal(barrier, p, col[k])
 
+    for load in loads:
+        load.start()
     for load in loads:
         load.wait()
     scale = f32(1.0 / math.sqrt(524288.0))
@@ -334,7 +333,7 @@
         kernel,
         out_shape=jax.ShapeDtypeStruct((32, 4096), f32),
         in_specs=[anywhere] * 3,
-        out_specs=anywhere,
+        out_specs=pl.BlockSpec(memory_space=pltpu.VMEM),
         scratch_shapes=[
             pltpu.VMEM((32, 4096), f32),
             pltpu.VMEM((1, 4096), i32),

time: 74.1 us -> 74.1 us (level)
  no operation moved by 1% of the time
where the time goes in v5:
time: 74.1 us; the launch traced here: 73.9 us
  Pallas kernels  70.6 us (95%)
  local copies, waits for them, and re-layouts  3.23 us (4%)
    pallas_call x1, Pallas kernels, shards(): pl.pallas_call(kernel, out_shape=jax.ShapeDtypeStruct((32, 4096), f32), i...  70.6 us
    unnamed x7, local copies, waits for them, and re-layouts  3.23 us

profile of v5, /device:TPU:1, one launch (start us, length us, event | category | flops | bytes accessed | tf_op | source)
XLA Modules:
  0.0 73.9 jit_solution(11657950557855147836)
XLA Ops:
  0.0 0.0 copy-start.2
  0.0 0.7 copy-done.2
  0.7 0.0 copy-start
  0.7 1.0 %copy-done = f32[32,4096]{1,0:T(8,128)S(1)} copy-done((f32[32,4096]{1,0:T(8,128)S(1)}, f32[32,4096]{1,0:T(8,128)}, u32[]{:S(2)}) %copy-start) | copy-done | bytes 524312
  1.7 0.0 copy-start.1
  1.7 0.7 copy-done.1
  2.4 70.6 %shard_map.37 = f32[32,4096]{1,0:T(8,128)S(1)} custom-call(f32[32,4096]{1,0:T(8,128)S(1)} %copy-done, s32[1,4096]{1,0:T(1,128)S(1)} %bitcast.2, s32[1,512]{1,0:T(1,128)S(1)} %bitcast.3), custom_call_target="tpu_custom_call" | custom-call | flops 1000000000 | bytes 1048576 | tf_op jit(solution)/shard_map/pallas_call | solution.py:332
  73.1 0.8 %copy.5 = f32[32,4096]{1,0:T(8,128)} copy(f32[32,4096]{1,0:T(8,128)S(1)} %shard_map.37) | data formatting | bytes 1048576
Async XLA Ops:
  0.0 0.7 copy-start.2
  0.7 1.0 %copy-start = (f32[32,4096]{1,0:T(8,128)S(1)}, f32[32,4096]{1,0:T(8,128)}, u32[]{:S(2)}) copy-start(f32[32,4096]{1,0:T(8,128)} %x_hbm.1) | copy-start | bytes 1572868
  1.7 0.7 copy-start.1
